TPU v7x, 128 devices: a whole 4x4x4 slice. The times are simulated.
128 devices in a mesh: grp: 4 (over y), blk: 32 (over x, z, core).
Axes of the slice: x: 4, y: 4, z: 4, core: 2. Of those that a mesh axis runs over, the one named last changes fastest.
Arguments:
- tiles: float32 [4096, 8, 128, 128], P(('grp', 'blk')), may hold values from -0.5 to 0.5
- coeffs: float32 [32768, 128], P('blk'), may hold values from -0.25 to 0.25
- domains: int32 [256, 128], P('blk'), may hold values 0 or 1
- tile_owner: int32 [4096, 1], P(('grp', 'blk')), may hold values from 0 to 31; in each aligned block of 32 rows (0 to 31, 32 to 63, ...) at most 2 rows name the same one
- tile_local: int32 [4096], P(('grp', 'blk')), may hold values from 0 to 7
- tile_aux: int32 [4096], P(('grp', 'blk')), may hold values from 0 to 3
- pair_owner: int32 [1152, 1], P('blk'), may hold values from 0 to 31; in each aligned block of 36 rows (0 to 35, 36 to 71, ...) at most 2 rows name the same one
Outputs:
- owned: float32 [2048, 128, 128], P('blk')
Inputs may be any that keep to these rules, and one draw needn't show every extreme that they name: `tile_owner`: in the rows of one device (aligned blocks of 32) no owner is named more than 2 times, a bound that some block reaches. `pair_owner`: in the rows of one device (aligned blocks of 36) no owner is named more than 2 times, a bound that some block reaches.
All inputs are finite; a program needn't handle non-finite values. No bound on the sum of `domains` on one device may be relied on, other than what follows from the above.
Results may differ from a plain program's by a relative error of at most 0.0003.
Values sent between devices are 32-bit elements; how exact they have to be, the bound alone decides.
A program may use at most 128 MiB of HBM per device.

v0:
```python
import jax
import jax.numpy as jnp
import numpy as np
from jax import lax
from jax.sharding import PartitionSpec as P

AB = 8
AUXG = 32
TPM = 4


HIGH = lax.Precision.HIGHEST


def pair_rank(owner):
    count = owner.shape[0]
    index = jnp.arange(count)
    same = (owner[:, None] == owner[None, :]) & (index[None, :] < index[:, None])
    return jnp.sum(same.astype(jnp.int32), axis=1)


def on_device(tiles, coeffs, domains, tile_owner, tile_local, tile_aux, pair_owner):
    nblk = lax.axis_size("blk")
    tile_count = tiles.shape[0]
    row_size = tiles.shape[2]
    occupied = coeffs.shape[1]
    blocks_here = domains.shape[0]
    owner = tile_owner[:, 0]
    gathered = lax.all_gather(coeffs, "blk", axis=0, tiled=True)
    gathered = gathered.reshape(nblk * blocks_here, row_size, occupied)
    source = owner * blocks_here + tile_local
    picked = gathered[source]
    products = jnp.einsum("eprs,esj->eprj", tiles, picked, precision=HIGH)
    naux = AUXG // AB
    local_block = jnp.arange(tile_count) // TPM
    which = local_block * naux + tile_aux
    onehot = (which[:, None] == jnp.arange(blocks_here * naux)[None, :]).astype(jnp.float32)
    factors = jnp.einsum("ek,eprj->kprj", onehot, products, precision=HIGH)
    factors = factors.reshape(blocks_here, AUXG, row_size, occupied)
    factors = factors * domains.astype(jnp.float32)[:, None, None, :]
    gram = jnp.einsum("aprj,bpsj->abrs", factors, factors, precision=HIGH)
    first_np, second_np = np.triu_indices(blocks_here)
    first = jnp.asarray(first_np.astype(np.int32))
    second = jnp.asarray(second_np.astype(np.int32))
    partial_value = gram[first, second]
    pair_count = partial_value.shape[0]
    capacity = max(2, (pair_count + nblk - 1) // nblk)
    targets = pair_owner[:, 0]
    pair_slot = (targets * capacity + pair_rank(targets)).astype(jnp.int32)
    placing = (jnp.arange(nblk * capacity).astype(jnp.int32)[:, None] == pair_slot[None, :]).astype(
        jnp.float32
    )
    outgoing = jnp.einsum("kq,qrs->krs", placing, partial_value, precision=HIGH)
    outgoing = outgoing.reshape(nblk, capacity, row_size, row_size)
    received = lax.all_to_all(outgoing, "blk", split_axis=0, concat_axis=0, tiled=True)
    received = lax.psum(received, "grp")
    return received.reshape(nblk * capacity, row_size, row_size)


def solution(mesh):
    placed = (
        P(("grp", "blk"), None, None, None),
        P("blk", None),
        P("blk", None),
        P(("grp", "blk"), None),
        P(("grp", "blk")),
        P(("grp", "blk")),
        P("blk", None),
    )
    return jax.shard_map(
        on_device, mesh=mesh, in_specs=placed, out_specs=P("blk", None, None), check_vma=False
    )
```

profile of v0, /device:TPU:1, one launch (start us, length us, event | category | flops | bytes accessed | tf_op | source)
XLA Modules:
  0.0 386.5 jit_solution(4384587564940728396)
XLA Ops:
  6.5 0.0 all-gather.2.cloned.1.call-start
  6.5 0.7 all-gather.2.cloned.1.call-update
  7.3 0.0 all-reduce.2.cloned.1.call-start
  7.3 0.7 convert_element_type.9
  8.0 0.7 compare_select_fusion
  8.7 0.9 convert_reduce_fusion
  9.6 0.7 fusion.21
  10.3 0.7 multiply_add_fusion
  10.9 75.0 %all-gather.2.cloned.1.call-done = f32[32768,128]{1,0:T(8,128)} async-done(((f32[1024,128]{1,0:T(8,128)}), f32[32768,128]{1,0:T(8,128)}) %all-gather.2.cloned.1.call-update) | async-done | bytes 16777232 | tf_op jit(solution)/shard_map/all_gather | solution.py:29
  85.9 6.4 %gather_fusion = f32[32,128,128]{2,1,0:T(8,128)S(1)} fusion(f32[256,128,128]{2,1,0:T(8,128)} %bitcast.75, s32[1024]{0:T(1024)S(1)} %pad_clamp_fusion), kind=kCustom, calls=%fused_computation | custom fusion | bytes 4194432 | tf_op jit(solution)/shard_map/gather | solution.py:32
  92.3 21.7 %convolution_bitcast_fusion = f32[32,8,128,128]{2,3,1,0:T(8,128)} fusion(f32[32,8,128,128]{3,2,1,0:T(8,128)} %param.9, f32[32,128,128]{2,1,0:T(8,128)S(1)} %gather_fusion), kind=kOutput, calls=%fused_computation.6 | convolution fusion | flops 6442450944 | bytes 35651584 | tf_op jit(solution)/shard_map/eprs,esj->eprj/dot_general | solution.py:33
  114.1 17.4 %copy.27 = f32[32,8,128,128]{3,0,2,1:T(8,128)} copy(f32[32,8,128,128]{2,3,1,0:T(8,128)} %convolution_bitcast_fusion) | data formatting | bytes 33554432 | tf_op jit(solution)/shard_map/eprs,esj->eprj/dot_general | solution.py:33
  131.4 14.9 %fusion.16 = f32[32,8,128,128]{3,0,2,1:T(8,128)} fusion(f32[32,8,128,128]{3,0,2,1:T(8,128)} %copy.27, s32[32]{0:T(128)S(1)} %fusion.21), kind=kOutput, calls=%fused_computation.19 | convolution fusion | flops 1610613760 | bytes 33554560 | tf_op jit(solution)/shard_map/ek,eprj->kprj/dot_general | solution.py:38
  146.3 9.4 %copy.28 = f32[32,8,128,128]{3,2,1,0:T(8,128)S(1)} copy(f32[32,8,128,128]{3,0,2,1:T(8,128)} %fusion.16) | data formatting | bytes 33554432 | tf_op jit(solution)/shard_map/ek,eprj->kprj/dot_general | solution.py:38
  155.7 56.2 %fusion.6 = f32[8,8,128,128]{2,3,1,0:T(8,128)} fusion(f32[8,128]{1,0:T(8,128)S(1)} %convert_element_type.9, f32[8,32,128,128]{3,2,1,0:T(8,128)S(1)} %bitcast.71, f32[8,32,128,128]{3,2,1,0:T(8,128)S(1)} %bitcast.72), kind=kOutput, calls=%fused_computation.10 | convolution fusion | flops 51547996160 | bytes 37752832 | tf_op jit(solution)/shard_map/aprj,bpsj->abrs/dot_general | solution.py:41
  211.9 0.0 copy-start
  211.9 5.4 %copy.29 = f32[8,8,128,128]{3,2,1,0:T(8,128)} copy(f32[8,8,128,128]{2,3,1,0:T(8,128)} %fusion.6) | data formatting | bytes 8388608 | tf_op jit(solution)/shard_map/aprj,bpsj->abrs/transpose | solution.py:41
  217.3 0.0 copy-done
  217.3 2.9 gather_fusion.1
  220.2 3.5 fusion.4
  223.7 2.3 copy.31
  226.0 55.8 %all_to_all.5 = f32[32,2,128,128]{3,1,2,0:T(2,128)S(1)} all-to-all(f32[32,2,128,128]{3,1,2,0:T(2,128)S(1)} %copy.31), channel_id=1, replica_groups=mesh['grp'=4,'blk'=32] {'blk'}, dimensions={0} | all-to-all | bytes 8388608 | tf_op jit(solution)/shard_map/all_to_all | solution.py:55
  281.8 2.6 copy.32
  284.4 0.0 all-reduce.2.cloned.1.call-update
  284.5 90.5 %all-reduce.2.cloned.1.call-done = f32[64,128,128]{2,1,0:T(8,128)} async-done(((f32[64,128,128]{2,1,0:T(8,128)}), f32[64,128,128]{2,1,0:T(8,128)}) %all-reduce.2.cloned.1.call-update) | async-done | bytes 4194320 | tf_op jit(solution)/shard_map/psum | solution.py:56
  375.0 4.7 %copy.42 = f32[64,128,128]{2,1,0:T(8,128)} copy(f32[64,128,128]{2,1,0:T(8,128)} %all-reduce.2.cloned.1.call-done) | data formatting | bytes 8388608
  (1 shorter events, 0.0 us)
Async XLA Ops:
  6.5 79.3 %all-gather.2.cloned.1.call-start = ((), (), s32[]{:S(2)}) async-start(), calls=%async_computation.1 | async-start | bytes 17301504 | tf_op jit(solution)/shard_map/all_gather | solution.py:29
  7.3 367.7 %all-reduce.2.cloned.1.call-start = ((), (), s32[]{:S(2)}) async-start(), calls=%async_computation.2 | async-start | bytes 8388608 | tf_op jit(solution)/shard_map/psum | solution.py:56
  211.9 5.4 %copy-start = (s32[36]{0:T(128)S(1)}, s32[36]{0:T(128)}, u32[]{:S(2)}) copy-start(s32[36]{0:T(128)} %constant.70) | copy-start | bytes 436
Sparse Core Ops, SparseCore 0:
  9.6 76.2 all-gather.1
  284.6 90.3 all-reduce.1
where the time goes:
time: 387 us
  waiting for transfers between devices  166 us (43%)
  matrix products  96.3 us (25%)
  blocking collectives  55.8 us (14%)
  local copies, waits for them, and re-layouts  51.1 us (13%)
  between operations  13.4 us (3%)
    psum x1, waiting for transfers between devices, on_device(): received = lax.psum(received, 'grp')  90.5 us
    all_gather x1, waiting for transfers between devices, on_device(): gathered = lax.all_gather(coeffs, 'blk', axis=0, tiled=True)  75 us
    dot_general x1, matrix products, on_device(): gram = jnp.einsum('aprj,bpsj->abrs', factors, factors, precision=HIGH)  56.2 us
    all_to_all x1, blocking collectives, on_device(): lax.all_to_all(outgoing, 'blk', split_axis=0, concat_axis=0, tiled=True)  55.8 us
    dot_general x1, matrix products, on_device(): products = jnp.einsum('eprs,esj->eprj', tiles, picked, precision=HIGH)  21.7 us
    dot_general x1, local copies, waits for them, and re-layouts, on_device(): products = jnp.einsum('eprs,esj->eprj', tiles, picked, precision=HIGH)  17.4 us
    dot_general x1, matrix products, on_device(): factors = jnp.einsum('ek,eprj->kprj', onehot, products, precision=HIGH)  14.9 us
    dot_general x1, local copies, waits for them, and re-layouts, on_device(): factors = jnp.einsum('ek,eprj->kprj', onehot, products, precision=HIGH)  9.4 us
  transfers between devices with their start and end apart: 2, of which 2 were waited for; matrix products, arithmetic and copies ran while one was open for 1% of the time, Pallas kernels for 0%

commit v1 on v0

v1 whole, which is shorter than its diff:
```python
import functools
import jax, jax.numpy as jnp
import numpy as np
from jax import lax
from jax.experimental import pallas as pl
from jax.experimental.pallas import tpu as pltpu
from jax.sharding import PartitionSpec as P

F32, BF16 = jnp.float32, jnp.bfloat16
NT = (((1,), (1,)), ((), ()))

def split(v):
    hi = v.astype(BF16)
    return hi, (v - hi.astype(F32)).astype(BF16)

def k2_body(src, aux, t, c0, c1, c2, c3, dom, out, F, H, L):
    m = pl.program_id(0)
    F[...] = jnp.zeros_like(F)
    for j, c in enumerate((c0, c1, c2, c3)):
        a = aux[m * 4 + j]
        ch, cl = split(c[0])
        w = jnp.concatenate([ch, cl], axis=1)
        w = jnp.concatenate([w, w], axis=0)
        for q in range(8):
            th, tl = split(t[j, q])
            p = jnp.dot(jnp.concatenate([th, tl], axis=1), w, preferred_element_type=F32)
            F[a, q] += p[:, :128] + p[:, 128:]
    mask = dom[0].astype(F32)
    rows = pl.ds(m * 128, 128)
    for a in range(4):
        for q in range(8):
            hi, lo = split(F[a, q] * mask)
            cols = pl.ds((a * 8 + q) * 128, 128)
            H[rows, cols] = hi
            L[rows, cols] = lo

    @pl.when(m == 7)
    def _():
        gram(out, H, L)

def gram(out, H, L):
    for J in range(4):
        @pl.loop(0, J + 1)
        def _(I):
            ri = pl.ds(I * 256, 256)
            rj = pl.ds(J * 256, 256)
            g = lax.dot_general(H[ri, :], H[rj, :], NT, preferred_element_type=F32)
            g += lax.dot_general(L[ri, :], H[rj, :], NT, preferred_element_type=F32)
            g += lax.dot_general(H[ri, :], L[rj, :], NT, preferred_element_type=F32)
            for x in range(2):
                mm = 2 * I + x
                base = mm * 8 - mm * (mm - 1) // 2 - mm
                for y in range(2):
                    nn = 2 * J + y
                    blk = g[x * 128:(x + 1) * 128, y * 128:(y + 1) * 128]
                    if x == 1 and y == 0:
                        @pl.when(I < J)
                        def _():
                            out[base + nn] = blk
                    else:
                        out[base + nn] = blk

def k2(tiles, coeffs, domains, source, aux):
    cs = [pl.BlockSpec((1, 128, 128), functools.partial(lambda j, m, s, a: (s[m * 4 + j], 0, 0), j)) for j in range(4)]
    return pl.pallas_call(
        k2_body,
        grid_spec=pltpu.PrefetchScalarGridSpec(
            num_scalar_prefetch=2, grid=(8,),
            in_specs=[pl.BlockSpec((4, 8, 128, 128), lambda m, s, a: (m, 0, 0, 0))] + cs +
                     [pl.BlockSpec((1, 1, 128), lambda m, s, a: (m, 0, 0))],
            out_specs=pl.BlockSpec((36, 128, 128), lambda m, s, a: (0, 0, 0)),
            scratch_shapes=[pltpu.VMEM((4, 8, 128, 128), F32), pltpu.VMEM((1024, 4096), BF16), pltpu.VMEM((1024, 4096), BF16)]),
        out_shape=jax.ShapeDtypeStruct((36, 128, 128), F32),
        compiler_params=pltpu.CompilerParams(vmem_limit_bytes=60 * 2**20),
        cost_estimate=pl.CostEstimate(flops=2 * 10**10, bytes_accessed=22 * 10**6, transcendentals=0),
    )(source, aux, tiles, coeffs, coeffs, coeffs, coeffs, domains)


def pair_rank(owner):
    index = jnp.arange(owner.shape[0])
    same = (owner[:, None] == owner[None, :]) & (index[None, :] < index[:, None])
    return jnp.sum(same.astype(jnp.int32), axis=1)


def on_device(tiles, coeffs, domains, tile_owner, tile_local, tile_aux, pair_owner):
    gathered = lax.all_gather(coeffs, "blk", axis=0, tiled=True).reshape(256, 128, 128)
    source = tile_owner[:, 0] * 8 + tile_local
    partial = k2(tiles, gathered, domains[:, None, :], source, tile_aux)
    targets = pair_owner[:, 0]
    slot = targets * 2 + pair_rank(targets)
    placing = (jnp.arange(64)[:, None] == slot[None, :]).astype(jnp.int32)
    used = jnp.sum(placing, axis=1)
    pair = jnp.sum(placing * jnp.arange(36)[None, :], axis=1)
    mine = lax.psum_scatter(partial, "grp", scatter_dimension=1, tiled=True)
    outgoing = jnp.where(used[:, None, None] > 0, mine[pair], 0.0)
    received = lax.all_to_all(outgoing, "blk", split_axis=0, concat_axis=0, tiled=True)
    return lax.all_gather(received, "grp", axis=1, tiled=True)


def solution(mesh):
    placed = (
        P(("grp", "blk"), None, None, None),
        P("blk", None),
        P("blk", None),
        P(("grp", "blk"), None),
        P(("grp", "blk")),
        P(("grp", "blk")),
        P("blk", None),
    )
    return jax.shard_map(
        on_device, mesh=mesh, in_specs=placed, out_specs=P("blk", None, None), check_vma=False
    )
```

time: 387 us -> 234 us (0.60)
  matrix products: 96.3 us -> 0 us
  local copies, waits for them, and re-layouts: 51.1 us -> 6.38 us
  Pallas kernels: 0 us -> 34.7 us
  blocking collectives: 55.8 us -> 24.4 us
  waiting for transfers between devices: 166 us -> 153 us
    dot_general x4 -> x0, matrix products: 96.3 us -> none  [the longest x1 56.2 us: on_device(): gram = jnp.einsum('aprj,bpsj->abrs', factors, factors, precision=HIGH)]
    psum x1 -> x0, waiting for transfers between devices: 90.5 us -> none  [on_device(): received = lax.psum(received, 'grp')]
    all_gather x1 -> x2, waiting for transfers between devices: 75 us -> 122 us  [the longest x1 77.4 us: on_device(): lax.all_gather(coeffs, 'blk', axis=0, tiled=True).reshape(256, 128, 128)]
    pallas_call x0 -> x1, Pallas kernels: none -> 34.7 us  [k2(): pl.pallas_call(k2_body, grid_spec=pltpu.PrefetchScalarGridSpec(num_scalar...]
    all_to_all x1, blocking collectives: 55.8 us -> 24.4 us  [on_device(): lax.all_to_all(outgoing, 'blk', split_axis=0, concat_axis=0, tiled=True)]
    reduce_scatter x0 -> x1, waiting for transfers between devices: none -> 30.6 us  [on_device(): mine = lax.psum_scatter(partial, 'grp', scatter_dimension=1, tiled=True)]
    dot_general x2 -> x0, local copies, waits for them, and re-layouts: 26.8 us -> none  [the longest x1 17.4 us: on_device(): products = jnp.einsum('eprs,esj->eprj', tiles, picked, precision=HIGH)]
    gather x2 -> x1, local copies, waits for them, and re-layouts: 9.36 us -> 1.68 us  [on_device(): outgoing = jnp.where(used[:, None, None] > 0, mine[pair], 0.0)]
  transfers between devices with their start and end apart: 2 -> 3, of which waited for: 2 -> 3; matrix products, arithmetic and copies ran while one was open for 1% -> 1% of each run, Pallas kernels for 0% -> 0%
where the time goes in v1:
time: 234 us
  waiting for transfers between devices  153 us (65%)
  Pallas kernels  34.7 us (15%)
  blocking collectives  24.4 us (10%)
  between operations  13.2 us (6%)
  local copies, waits for them, and re-layouts  6.38 us (3%)
    all_gather x1, waiting for transfers between devices, on_device(): lax.all_gather(coeffs, 'blk', axis=0, tiled=True).reshape(256, 128, 128)  77.4 us
    all_gather x1, waiting for transfers between devices, on_device(): return lax.all_gather(received, 'grp', axis=1, tiled=True)  44.4 us
    pallas_call x1, Pallas kernels, k2(): pl.pallas_call(k2_body, grid_spec=pltpu.PrefetchScalarGridSpec(num_scalar...  34.7 us
    reduce_scatter x1, waiting for transfers between devices, on_device(): mine = lax.psum_scatter(partial, 'grp', scatter_dimension=1, tiled=True)  30.6 us
    all_to_all x1, blocking collectives, on_device(): lax.all_to_all(outgoing, 'blk', split_axis=0, concat_axis=0, tiled=True)  24.4 us
    unnamed x3, local copies, waits for them, and re-layouts  4.7 us
  transfers between devices with their start and end apart: 3, of which 3 were waited for; matrix products, arithmetic and copies ran while one was open for 1% of the time, Pallas kernels for 0%

profile of v1, /device:TPU:1, one launch (start us, length us, event | category | flops | bytes accessed | tf_op | source)
XLA Modules:
  0.0 233.5 jit_solution(2270340864760025635)
XLA Ops:
  6.5 0.0 all-gather.3.cloned.1.call-start
  6.5 0.7 all-gather.3.cloned.1.call-update
  7.3 0.0 reduce-scatter.2.cloned.1.call-start
  7.3 1.2 bitcast_add_fusion.src
  8.5 77.4 %all-gather.3.cloned.1.call-done = f32[32768,128]{1,0:T(8,128)} async-done(((f32[1024,128]{1,0:T(8,128)}), f32[32768,128]{1,0:T(8,128)}) %all-gather.3.cloned.1.call-update) | async-done | bytes 16777232 | tf_op jit(solution)/shard_map/all_gather | solution.py:86
  85.9 0.0 copy-start
  85.9 34.7 %shard_map.73 = f32[36,128,128]{2,1,0:T(8,128)} custom-call(s32[32]{0:T(128)} %bitcast_add_fusion.src, s32[32]{0:T(128)} %aux.1, f32[32,8,128,128]{3,2,1,0:T(8,128)} %t.1, f32[256,128,128]{2,1,0:T(8,128)} %bitcast.10, f32[256,128,128]{2,1,0:T(8,128)} %bitcast.11, f32[256,128,128]{2,1,0:T(8,128)} %bitcast.12, f32[256,128,128]{2,1,0:T(8,128)} %bitcast.13, ...), custom_call_target="tpu_custom_call" | custom-call | flops 20000000000 | bytes 22000000 | tf_op jit(solution)/shard_map/pallas_call | solution.py:65
  120.6 0.0 reduce-scatter.2.cloned.1.call-update
  120.6 0.0 all-gather.5.cloned.1.call-start
  120.7 0.0 copy-done
  120.7 0.2 convert_reduce_fusion.1
  120.9 0.1 convert_reduce_fusion
  121.0 30.6 %reduce-scatter.2.cloned.1.call-done = f32[36,32,128]{2,1,0:T(8,128)} async-done(((f32[36,128,128]{2,1,0:T(8,128)}), f32[36,32,128]{2,1,0:T(8,128)}) %reduce-scatter.2.cloned.1.call-update) | async-done | bytes 589840 | tf_op jit(solution)/shard_map/reduce_scatter | solution.py:94
  151.6 1.7 gather_fusion
  153.3 0.1 broadcast_select_fusion
  153.5 24.4 %all_to_all.5 = f32[64,32,128]{2,1,0:T(8,128)} all-to-all(f32[64,32,128]{2,1,0:T(8,128)S(1)} %broadcast_select_fusion), channel_id=1, replica_groups=mesh['grp'=4,'blk'=32] {'blk'}, dimensions={0} | all-to-all | bytes 2097152 | tf_op jit(solution)/shard_map/all_to_all | solution.py:96
  177.9 0.0 all-gather.5.cloned.1.call-update
  177.9 44.4 %all-gather.5.cloned.1.call-done = f32[64,128,128]{2,1,0:T(8,128)} async-done(((f32[64,32,128]{2,1,0:T(8,128)}), f32[64,128,128]{2,1,0:T(8,128)}) %all-gather.5.cloned.1.call-update) | async-done | bytes 4194320 | tf_op jit(solution)/shard_map/all_gather | solution.py:97
  222.3 4.7 %copy.9 = f32[64,128,128]{2,1,0:T(8,128)} copy(f32[64,128,128]{2,1,0:T(8,128)} %all-gather.5.cloned.1.call-done) | data formatting | bytes 8388608
  (4 shorter events, 0.0 us)
Async XLA Ops:
  6.5 79.3 %all-gather.3.cloned.1.call-start = ((), (), s32[]{:S(2)}) async-start(), calls=%async_computation.2 | async-start | bytes 17301504 | tf_op jit(solution)/shard_map/all_gather | solution.py:86
  7.3 144.4 %reduce-scatter.2.cloned.1.call-start = ((), (), s32[]{:S(2)}) async-start(), calls=%async_computation.3 | async-start | bytes 2949120 | tf_op jit(solution)/shard_map/reduce_scatter | solution.py:94
  85.9 34.8 %copy-start = (s32[36,1]{0,1:T(1,128)S(1)}, s32[36,1]{0,1:T(1,128)}, u32[]{:S(2)}) copy-start(s32[36,1]{0,1:T(1,128)} %param.13) | copy-start | bytes 436
  120.6 101.7 %all-gather.5.cloned.1.call-start = ((), (), s32[]{:S(2)}) async-start(), calls=%async_computation.4 | async-start | bytes 5242880 | tf_op jit(solution)/shard_map/all_gather | solution.py:97
Sparse Core Ops, SparseCore 0:
  9.6 76.2 all-gather.2
  120.7 30.8 reduce-scatter.1
  178.0 44.2 all-gather.4

commit v2 on v1

--- a/solution.py
+++ b/solution.py
@@ -1,6 +1,5 @@
 import functools
 import jax, jax.numpy as jnp
-import numpy as np
 from jax import lax
 from jax.experimental import pallas as pl
 from jax.experimental.pallas import tpu as pltpu
@@ -8,6 +7,9 @@
 
 F32, BF16 = jnp.float32, jnp.bfloat16
 NT = (((1,), (1,)), ((), ()))
+
+MESH = pl.DeviceIdType.MESH
+
 
 def split(v):
     hi = v.astype(BF16)
@@ -76,6 +78,267 @@
     )(source, aux, tiles, coeffs, coeffs, coeffs, coeffs, domains)
 
 
+def coords():
+    b = lax.axis_index("blk")
+    y = lax.axis_index("grp")
+    return b // 8, y, lax.rem(b // 2, 4), lax.rem(b, 2)
+
+
+def index(x, z, c):
+    return (lax.rem(x + 8, 4) * 4 + lax.rem(z + 8, 4)) * 2 + c
+
+
+def enter(partners):
+    barrier = pltpu.get_barrier_semaphore()
+    for g, b in partners:
+        pl.semaphore_signal(barrier, inc=1, device_id={"grp": g, "blk": b}, device_id_type=MESH)
+    pl.semaphore_wait(barrier, len(partners))
+
+
+def gather_body(own, out, send, recv, sib_send, sib_recv, local_sem):
+    x, y, z, c = coords()
+    me = index(x, z, c)
+    other = index(x, z, 1 - c)
+    axes = [((1, 0), (0, 1)), ((0, 1), (1, 0))]
+
+    def at(part, du, dv):
+        (ux, uz), (vx, vz) = axes[part]
+        return index(x + du * ux + dv * vx, z + du * uz + dv * vz, c)
+
+    enter([(y, index(x + 1, z, c)), (y, index(x - 1, z, c)), (y, index(x, z + 1, c)), (y, index(x, z - 1, c)), (y, other)])
+    here = pltpu.make_async_copy(own, out.at[me], local_sem)
+    here.start()
+    sends, sibs = [], []
+    count = [0, 0]
+
+    def remote(src, dst, to, k):
+        cp = pltpu.make_async_remote_copy(src_ref=src, dst_ref=dst, send_sem=send.at[k], recv_sem=recv.at[k],
+                                          device_id={"grp": y, "blk": to}, device_id_type=MESH)
+        return cp
+
+    def sibling(src_dev, lo, n, src=None, other_dev=None):
+        k = count[1]
+        count[1] += 1
+        ref = out.at[src_dev, pl.ds(lo, n)] if src is None else src
+        cp = pltpu.make_async_remote_copy(src_ref=ref, dst_ref=out.at[src_dev, pl.ds(lo, n)], send_sem=sib_send.at[k],
+                                          recv_sem=sib_recv.at[k], device_id={"grp": y, "blk": other}, device_id_type=MESH)
+        cp.start()
+        sibs.append((k, src_dev, lo, n, cp))
+
+    table = {}
+
+    def define(part, key, du, dv, lo, n):
+        table[part, key] = (len(table), du, dv, part * 4 + lo, n)
+
+    for part in range(2):
+        define(part, "u+", -1, 0, 0, 4)
+        define(part, "u-", 1, 0, 0, 4)
+        define(part, "uu+", -2, 0, 0, 2)
+        define(part, "uu-", 2, 0, 2, 2)
+        for sign in (1, -1):
+            for name, du, lo, n in (("0", 0, 0, 4), ("m", -1, 0, 4), ("p", 1, 0, 4), ("2l", 2, 0, 2), ("2h", 2, 2, 2)):
+                define(part, ("v", sign, name), du, -sign, lo, n)
+            for name, du in (("0", 0), ("m", -1), ("p", 1), ("2", 2)):
+                define(part, ("vv", sign, name), du, -2 * sign, 0 if sign > 0 else 2, 2)
+
+    def post(part, key, du_to, dv_to, src=None):
+        k, du, dv, lo, n = table[part, key]
+        source = at(part, du + du_to, dv + dv_to)
+        region = out.at[source, pl.ds(lo, n)]
+        cp = remote(region if src is None else src.at[pl.ds(lo, n)], region, at(part, du_to, dv_to), k)
+        cp.start()
+        sends.append(cp)
+
+    def arrive(part, key, share=True):
+        k, du, dv, lo, n = table[part, key]
+        source = at(part, du, dv)
+        region = out.at[source, pl.ds(lo, n)]
+        remote(region, region, at(part, 0, 0), k).wait_recv()
+        if share:
+            sibling(source, lo, n)
+
+    for part in range(2):
+        post(part, "u+", 1, 0, own)
+        post(part, "u-", -1, 0, own)
+    for part in range(2):
+        post(part, ("v", 1, "0"), 0, 1, own)
+        post(part, ("v", -1, "0"), 0, -1, own)
+    sibling(me, 0, 8, own)
+    for key, name, fwd, step in (("u+", "m", "uu+", 1), ("u-", "p", "uu-", -1)):
+        for part in range(2):
+            arrive(part, key)
+            post(part, fwd, step, 0)
+            post(part, ("v", 1, name), 0, 1)
+            post(part, ("v", -1, name), 0, -1)
+    for sign in (1, -1):
+        for part in range(2):
+            arrive(part, ("v", sign, "0"))
+            post(part, ("vv", sign, "0"), 0, sign)
+    for key, name in (("uu+", "2l"), ("uu-", "2h")):
+        for part in range(2):
+            arrive(part, key)
+            post(part, ("v", 1, name), 0, 1)
+            post(part, ("v", -1, name), 0, -1)
+    for name in ("m", "p"):
+        for sign in (1, -1):
+            for part in range(2):
+                arrive(part, ("v", sign, name))
+                post(part, ("vv", sign, name), 0, sign)
+    for sign, name, drop in ((1, "2l", "2h"), (-1, "2h", "2l")):
+        for part in range(2):
+            arrive(part, ("v", sign, name))
+            post(part, ("vv", sign, "2"), 0, sign)
+            arrive(part, ("v", -sign, name))
+    for name in ("0", "m", "p", "2"):
+        for sign in (1, -1):
+            for part in range(2):
+                arrive(part, ("vv", sign, name))
+    here.wait()
+    for k, src_dev, lo, n, cp in sibs:
+        theirs = src_dev + 1 - 2 * c
+        region = out.at[theirs, pl.ds(lo, n)]
+        pltpu.make_async_remote_copy(src_ref=region, dst_ref=region, send_sem=sib_send.at[k], recv_sem=sib_recv.at[k],
+                                     device_id={"grp": y, "blk": other}, device_id_type=MESH).wait_recv()
+        cp.wait_send()
+    for cp in sends:
+        cp.wait_send()
+
+
+def gather(coeffs):
+    return pl.pallas_call(
+        gather_body,
+        out_shape=jax.ShapeDtypeStruct((32, 8, 128, 128), F32),
+        in_specs=[pl.BlockSpec(memory_space=pl.ANY)],
+        out_specs=pl.BlockSpec(memory_space=pl.ANY),
+        scratch_shapes=[pltpu.SemaphoreType.DMA((44,)), pltpu.SemaphoreType.DMA((44,)), pltpu.SemaphoreType.DMA((45,)),
+                        pltpu.SemaphoreType.DMA((45,)), pltpu.SemaphoreType.DMA],
+        compiler_params=pltpu.CompilerParams(collective_id=1, has_side_effects=True),
+    )(coeffs.reshape(8, 128, 128))
+
+
+def exchange_body(partial, pair, used, out, sums, placed, got, take, rs_send, rs_recv, a_send, a_recv, g_send, g_recv, local_sem):
+    x, y, z, c = coords()
+    me = index(x, z, c)
+
+    def plane(d):
+        return lax.rem(y + d + 4, 4)
+
+    def peer(dx, d):
+        return index(x + dx, z + d // 2, lax.rem(c + d, 2))
+
+    barrier = pltpu.get_barrier_semaphore()
+    for d in (1, 2, 3):
+        pl.semaphore_signal(barrier, inc=1, device_id={"grp": plane(d), "blk": me}, device_id_type=MESH)
+
+    @pl.loop(1, 32)
+    def _(k):
+        pl.semaphore_signal(barrier, inc=1, device_id={"grp": y, "blk": peer(k // 8, lax.rem(k, 8))}, device_id_type=MESH)
+
+    pl.semaphore_wait(barrier, 34)
+
+    rs = []
+    for d in (1, 3, 2):
+        cp = pltpu.make_async_remote_copy(
+            src_ref=partial.at[:, pl.ds(32 * plane(d), 32), :], dst_ref=sums.at[d - 1], send_sem=rs_send.at[d - 1],
+            recv_sem=rs_recv.at[d - 1], device_id={"grp": plane(d), "blk": me}, device_id_type=MESH)
+        cp.start()
+        rs.append(cp)
+    for cp in rs:
+        cp.wait_recv()
+
+    @pl.loop(0, 36)
+    def _(q):
+        take[q] = (partial[q, pl.ds(32 * y, 32), :] + sums[0, q]) + (sums[1, q] + sums[2, q])
+
+    @pl.loop(0, 64)
+    def _(s):
+        placed[s] = take[pair[s]] * used[s].astype(F32)
+
+    def shipment(dx, d):
+        to = peer(dx, d)
+        return pltpu.make_async_remote_copy(
+            src_ref=placed.at[pl.ds(2 * to, 2)], dst_ref=got.at[pl.ds(2 * me, 2)], send_sem=a_send.at[dx, d],
+            recv_sem=a_recv.at[dx, d], device_id={"grp": y, "blk": to}, device_id_type=MESH)
+
+    def arrival(dx, d):
+        frm = index(x - dx, z - d // 2 + 4, lax.rem(c + d, 2))
+        region = got.at[pl.ds(2 * frm, 2)]
+        return pltpu.make_async_remote_copy(
+            src_ref=region, dst_ref=region, send_sem=a_send.at[dx, d], recv_sem=a_recv.at[dx, d],
+            device_id={"grp": y, "blk": me}, device_id_type=MESH)
+
+    for dx in (0, 1, 3, 2):
+        @pl.loop(1 if dx == 0 else 0, 8)
+        def _(d):
+            shipment(dx, d).start()
+    mine = pltpu.make_async_copy(placed.at[pl.ds(2 * me, 2)], got.at[pl.ds(2 * me, 2)], local_sem.at[4])
+    mine.start()
+    mine.wait()
+
+    def rows(plane_index):
+        return pl.ds(32 * plane_index, 32)
+
+    sends, locals_ = [], []
+    for dx in (0, 1, 3, 2):
+        @pl.loop(1 if dx == 0 else 0, 8)
+        def _(d):
+            arrival(dx, d).wait_recv()
+        first = 16 * lax.rem(x - dx + 4, 4)
+        for i, step in enumerate((1, -1)):
+            cp = pltpu.make_async_remote_copy(
+                src_ref=got.at[pl.ds(first, 16)], dst_ref=out.at[pl.ds(first, 16), rows(y)], send_sem=g_send.at[dx, i],
+                recv_sem=g_recv.at[dx, i], device_id={"grp": plane(step), "blk": me}, device_id_type=MESH)
+            cp.start()
+            sends.append(cp)
+        cp = pltpu.make_async_copy(got.at[pl.ds(first, 16)], out.at[pl.ds(first, 16), rows(y)], local_sem.at[dx])
+        cp.start()
+        locals_.append(cp)
+    for dx in (0, 1, 3, 2):
+        first = 16 * lax.rem(x - dx + 4, 4)
+        for i, step in enumerate((1, -1)):
+            region = out.at[pl.ds(first, 16), rows(plane(-step))]
+            pltpu.make_async_remote_copy(
+                src_ref=region, dst_ref=region, send_sem=g_send.at[dx, i], recv_sem=g_recv.at[dx, i],
+                device_id={"grp": y, "blk": me}, device_id_type=MESH).wait_recv()
+            half = out.at[pl.ds(first + 8 * i, 8), rows(plane(-step))]
+            cp = pltpu.make_async_remote_copy(
+                src_ref=half, dst_ref=half, send_sem=g_send.at[dx, 2 + i], recv_sem=g_recv.at[dx, 2 + i],
+                device_id={"grp": plane(step), "blk": me}, device_id_type=MESH)
+            cp.start()
+            sends.append(cp)
+    for dx in (0, 1, 3, 2):
+        first = 16 * lax.rem(x - dx + 4, 4)
+        for i in range(2):
+            half = out.at[pl.ds(first + 8 * i, 8), rows(plane(2))]
+            pltpu.make_async_remote_copy(
+                src_ref=half, dst_ref=half, send_sem=g_send.at[dx, 2 + i], recv_sem=g_recv.at[dx, 2 + i],
+                device_id={"grp": y, "blk": me}, device_id_type=MESH).wait_recv()
+    for cp in locals_:
+        cp.wait()
+    for cp in rs + sends:
+        cp.wait_send()
+    for dx in range(4):
+        @pl.loop(1 if dx == 0 else 0, 8)
+        def _(d):
+            shipment(dx, d).wait_send()
+
+
+def exchange(partial, pair, used):
+    vm = pl.BlockSpec(memory_space=pltpu.VMEM)
+    sm = pl.BlockSpec(memory_space=pltpu.SMEM)
+    dma = pltpu.SemaphoreType.DMA
+    return pl.pallas_call(
+        exchange_body,
+        out_shape=jax.ShapeDtypeStruct((64, 128, 128), F32),
+        in_specs=[vm, sm, sm],
+        out_specs=pl.BlockSpec(memory_space=pl.ANY),
+        scratch_shapes=[pltpu.VMEM((3, 36, 32, 128), F32), pltpu.VMEM((64, 32, 128), F32), pltpu.VMEM((64, 32, 128), F32),
+                        pltpu.VMEM((36, 32, 128), F32),
+                        dma((3,)), dma((3,)), dma((4, 8)), dma((4, 8)), dma((4, 4)), dma((4, 4)), dma((5,))],
+        compiler_params=pltpu.CompilerParams(collective_id=2, has_side_effects=True, vmem_limit_bytes=32 * 2**20),
+    )(partial, pair, used)
+
+
 def pair_rank(owner):
     index = jnp.arange(owner.shape[0])
     same = (owner[:, None] == owner[None, :]) & (index[None, :] < index[:, None])
@@ -83,7 +346,7 @@
 
 
 def on_device(tiles, coeffs, domains, tile_owner, tile_local, tile_aux, pair_owner):
-    gathered = lax.all_gather(coeffs, "blk", axis=0, tiled=True).reshape(256, 128, 128)
+    gathered = gather(coeffs).reshape(256, 128, 128)
     source = tile_owner[:, 0] * 8 + tile_local
     partial = k2(tiles, gathered, domains[:, None, :], source, tile_aux)
     targets = pair_owner[:, 0]
@@ -91,10 +354,7 @@
     placing = (jnp.arange(64)[:, None] == slot[None, :]).astype(jnp.int32)
     used = jnp.sum(placing, axis=1)
     pair = jnp.sum(placing * jnp.arange(36)[None, :], axis=1)
-    mine = lax.psum_scatter(partial, "grp", scatter_dimension=1, tiled=True)
-    outgoing = jnp.where(used[:, None, None] > 0, mine[pair], 0.0)
-    received = lax.all_to_all(outgoing, "blk", split_axis=0, concat_axis=0, tiled=True)
-    return lax.all_gather(received, "grp", axis=1, tiled=True)
+    return exchange(partial, pair, used)
 
 
 def solution(mesh):

time: 234 us -> 177 us (0.76)
  waiting for transfers between devices: 153 us -> 0 us
  Pallas kernels: 34.7 us -> 171 us
  blocking collectives: 24.4 us -> 0 us
  between operations: 13.2 us -> 0.04 us
  local copies, waits for them, and re-layouts: 6.38 us -> 3.69 us
    pallas_call x0 -> x2, Pallas kernels: none -> 137 us  [the longest x1 82 us: exchange(): pl.pallas_call(exchange_body, out_shape=jax.ShapeDtypeStruct((64, 128, 12...]
    all_gather x2 -> x0, waiting for transfers between devices: 122 us -> none  [the longest x1 77.4 us: on_device(): lax.all_gather(coeffs, 'blk', axis=0, tiled=True).reshape(256, 128, 128)]
    reduce_scatter x1 -> x0, waiting for transfers between devices: 30.6 us -> none  [on_device(): mine = lax.psum_scatter(partial, 'grp', scatter_dimension=1, tiled=True)]
    all_to_all x1 -> x0, blocking collectives: 24.4 us -> none  [on_device(): lax.all_to_all(outgoing, 'blk', split_axis=0, concat_axis=0, tiled=True)]
    unnamed x3 -> x5, local copies, waits for them, and re-layouts: 4.7 us -> 3.69 us
  transfers between devices with their start and end apart: 3 -> 0, of which waited for: 3 -> 0; matrix products, arithmetic and copies ran while one was open for 1% -> 0% of each run, Pallas kernels for 0% -> 0%
where the time goes in v2:
time: 177 us; the launch traced here: 176 us
  Pallas kernels  171 us (97%)
  local copies, waits for them, and re-layouts  3.69 us (2%)
    pallas_call x1, Pallas kernels, exchange(): pl.pallas_call(exchange_body, out_shape=jax.ShapeDtypeStruct((64, 128, 12...  82 us
    pallas_call x1, Pallas kernels, gather(): pl.pallas_call(gather_body, out_shape=jax.ShapeDtypeStruct((32, 8, 128, 1...  54.6 us
    pallas_call x1, Pallas kernels, k2(): pl.pallas_call(k2_body, grid_spec=pltpu.PrefetchScalarGridSpec(num_scalar...  34.6 us
    unnamed x5, local copies, waits for them, and re-layouts  3.69 us

profile of v2, /device:TPU:1, one launch (start us, length us, event | category | flops | bytes accessed | tf_op | source)
XLA Modules:
  0.0 176.3 jit_solution(17832706226475692698)
XLA Ops:
  0.0 1.2 bitcast_add_fusion.src
  1.2 54.6 %shard_map.73 = f32[32,8,128,128]{3,2,1,0:T(8,128)} custom-call(f32[8,128,128]{2,1,0:T(8,128)} %bitcast.11), custom_call_target="tpu_custom_call" | custom-call | tf_op jit(solution)/shard_map/pallas_call | solution.py:208
  55.8 0.0 copy-start.1
  55.8 34.6 %shard_map.74.partial = f32[36,128,128]{2,1,0:T(8,128)} custom-call(s32[32]{0:T(128)} %bitcast_add_fusion.src, s32[32]{0:T(128)} %aux.1, f32[32,8,128,128]{3,2,1,0:T(8,128)} %t.1, f32[256,128,128]{2,1,0:T(8,128)} %bitcast.7, f32[256,128,128]{2,1,0:T(8,128)} %bitcast.8, f32[256,128,128]{2,1,0:T(8,128)} %bitcast.9, f32[256,128,128]{2,1,0:T(8,128)} %bitcast.10, ...), custom_call_target="tpu_custom_call" | custom-call | flops 20000000000 | bytes 22000000 | tf_op jit(solution)/shard_map/pallas_call | solution.py:67
  90.3 0.0 copy-done.1
  90.4 0.2 convert_reduce_fusion.1
  90.5 0.1 convert_reduce_fusion
  90.6 0.0 copy-start
  90.6 1.7 copy-done
  92.3 82.0 %shard_map.75 = f32[64,128,128]{2,1,0:T(8,128)S(1)} custom-call(f32[36,128,128]{2,1,0:T(8,128)S(1)} %copy-done, s32[64]{0:T(128)S(1)} %get-tuple-element.6.pair, s32[64]{0:T(128)S(1)} %get-tuple-element.5.used), custom_call_target="tpu_custom_call" | custom-call | tf_op jit(solution)/shard_map/pallas_call | solution.py:330
  174.3 2.0 %copy.9 = f32[64,128,128]{2,1,0:T(8,128)} copy(f32[64,128,128]{2,1,0:T(8,128)S(1)} %shard_map.75) | data formatting | bytes 8388608
  (1 shorter events, 0.0 us)
Async XLA Ops:
  55.8 34.6 %copy-start.1 = (s32[36,1]{0,1:T(1,128)S(1)}, s32[36,1]{0,1:T(1,128)}, u32[]{:S(2)}) copy-start(s32[36,1]{0,1:T(1,128)} %param.13) | copy-start | bytes 436
  90.6 1.7 copy-start

commit v3 on v0

v3 whole, which is shorter than its diff:
```python
import jax
import jax.numpy as jnp
import numpy as np
from jax import lax
from jax.experimental import pallas as pl
from jax.experimental.pallas import tpu as pltpu
from jax.sharding import PartitionSpec as P

F32, BF16 = jnp.float32, jnp.bfloat16
MESH = pl.DeviceIdType.MESH
NT = (((1,), (1,)), ((), ()))
CHUNKS = ((0, 8), (8, 7), (15, 8), (23, 6), (29, 7))


def places():
    spot = {}
    for m in range(4):
        for n in (6, 7):
            spot[m, n] = (n - 6) * 4 + m
        for n in (4, 5):
            spot[m, n] = 15 + (n - 4) * 4 + m
    for m in range(4, 8):
        for n in (6, 7):
            spot[m, n] = 8 + 3 * (n - 6) + m - 4
    for s, m in ((0, 4), (1, 0)):
        spot[m, m], spot[m, m + 1], spot[m + 1, m + 1] = 23 + 3 * s, 24 + 3 * s, 25 + 3 * s
    for m in range(4):
        for n in (2, 3):
            spot[m, n] = 29 + 3 * (n - 2) + m
    return np.array([spot[m, n] for m in range(8) for n in range(m, 8)], np.int32)


def split(v):
    hi = v.astype(BF16)
    return hi, (v - hi.astype(F32)).astype(BF16)


def coords():
    b = lax.axis_index("blk")
    return b // 8, lax.axis_index("grp"), lax.rem(b // 2, 4), lax.rem(b, 2)


def index(x, z, c):
    return (lax.rem(x + 8, 4) * 4 + lax.rem(z + 8, 4)) * 2 + c


def gather_coeffs(own, coef, sems, work):
    send, recv, sib_send, sib_recv, local_sem = sems
    x, y, z, c = coords()
    me = index(x, z, c)
    other = index(x, z, 1 - c)
    axes = [((1, 0), (0, 1)), ((0, 1), (1, 0))]

    def at(part, du, dv):
        (ux, uz), (vx, vz) = axes[part]
        return index(x + du * ux + dv * vx, z + du * uz + dv * vz, c)

    here = pltpu.make_async_copy(own, coef.at[me], local_sem)
    here.start()
    sends, sibs = [], []

    def remote(src, dst, to, s, r):
        return pltpu.make_async_remote_copy(src_ref=src, dst_ref=dst, send_sem=s, recv_sem=r,
                                            device_id={"grp": y, "blk": to}, device_id_type=MESH)

    def sibling(source, lo, n, src=None):
        k = len(sibs)
        region = coef.at[source, pl.ds(lo, n)]
        cp = remote(region if src is None else src, region, other, sib_send.at[k], sib_recv.at[k])
        cp.start()
        sibs.append((source, lo, n, cp))

    table = {}

    def define(part, key, du, dv, lo, n):
        table[part, key] = (len(table), du, dv, part * 4 + lo, n)

    for part in range(2):
        define(part, "u+", -1, 0, 0, 4)
        define(part, "u-", 1, 0, 0, 4)
        define(part, "uu+", -2, 0, 0, 2)
        define(part, "uu-", 2, 0, 2, 2)
        for sign in (1, -1):
            for name, du, lo, n in (("0", 0, 0, 4), ("m", -1, 0, 4), ("p", 1, 0, 4), ("2l", 2, 0, 2), ("2h", 2, 2, 2)):
                define(part, ("v", sign, name), du, -sign, lo, n)
            for name, du in (("0", 0), ("m", -1), ("p", 1), ("2", 2)):
                define(part, ("vv", sign, name), du, -2 * sign, 0 if sign > 0 else 2, 2)

    def post(part, key, du_to, dv_to, src=None):
        k, du, dv, lo, n = table[part, key]
        region = coef.at[at(part, du + du_to, dv + dv_to), pl.ds(lo, n)]
        cp = remote(region if src is None else src.at[pl.ds(lo, n)], region, at(part, du_to, dv_to), send.at[k], recv.at[k])
        cp.start()
        sends.append(cp)

    def arrive(part, key):
        k, du, dv, lo, n = table[part, key]
        source = at(part, du, dv)
        region = coef.at[source, pl.ds(lo, n)]
        remote(region, region, me, send.at[k], recv.at[k]).wait_recv()
        sibling(source, lo, n)

    def meanwhile():
        if work:
            work.pop(0)()

    for part in range(2):
        post(part, "u+", 1, 0, own)
        post(part, "u-", -1, 0, own)
    for part in range(2):
        post(part, ("v", 1, "0"), 0, 1, own)
        post(part, ("v", -1, "0"), 0, -1, own)
    sibling(me, 0, 8, own)
    meanwhile()
    meanwhile()
    for key, name, fwd, step in (("u+", "m", "uu+", 1), ("u-", "p", "uu-", -1)):
        for part in range(2):
            arrive(part, key)
            post(part, fwd, step, 0)
            post(part, ("v", 1, name), 0, 1)
            post(part, ("v", -1, name), 0, -1)
    meanwhile()
    for sign in (1, -1):
        for part in range(2):
            arrive(part, ("v", sign, "0"))
            post(part, ("vv", sign, "0"), 0, sign)
    meanwhile()
    for key, name in (("uu+", "2l"), ("uu-", "2h")):
        for part in range(2):
            arrive(part, key)
            post(part, ("v", 1, name), 0, 1)
            post(part, ("v", -1, name), 0, -1)
    meanwhile()
    for name in ("m", "p"):
        for sign in (1, -1):
            for part in range(2):
                arrive(part, ("v", sign, name))
                post(part, ("vv", sign, name), 0, sign)
        meanwhile()
    for sign, name, drop in ((1, "2l", "2h"), (-1, "2h", "2l")):
        for part in range(2):
            arrive(part, ("v", sign, name))
            post(part, ("vv", sign, "2"), 0, sign)
            arrive(part, ("v", -sign, name))
    while work:
        meanwhile()
    for name in ("0", "m", "p", "2"):
        for sign in (1, -1):
            for part in range(2):
                arrive(part, ("vv", sign, name))
    here.wait()
    for k, (source, lo, n, cp) in enumerate(sibs):
        region = coef.at[source + 1 - 2 * c, pl.ds(lo, n)]
        remote(region, region, me, sib_send.at[k], sib_recv.at[k]).wait_recv()
    for cp in sends + [s[3] for s in sibs]:
        cp.wait_send()


def body(own, tiles, owner, local, aux, dom, pair, used, out,
         coef, halves, stage, H, L, partial, sums, take, both, placed1, got,
         g1s, g1r, sbs, sbr, one_sem, st_sem, rs_s, rs_r, b_s, b_r, a1_s, a1_r, a2_s, a2_r, w_s, w_r, loc):
    placed2 = stage.at[1]
    x, y, z, c = coords()
    me = index(x, z, c)

    def plane(d):
        return lax.rem(y + d + 4, 4)

    def peer(dx, d):
        return index(x + dx, z + d // 2, lax.rem(c + d, 2))

    def remote(src, dst, s, r, g, b):
        return pltpu.make_async_remote_copy(src_ref=src, dst_ref=dst, send_sem=s, recv_sem=r,
                                            device_id={"grp": g, "blk": b}, device_id_type=MESH)

    def fetch(m):
        return pltpu.make_async_copy(tiles.at[pl.ds(4 * m, 4)], stage.at[m % 2], st_sem.at[m])

    fetch(0).start()
    fetch(1).start()
    barrier = pltpu.get_barrier_semaphore()
    for d in (1, 2, 3):
        pl.semaphore_signal(barrier, inc=1, device_id={"grp": plane(d), "blk": me}, device_id_type=MESH)

    @pl.loop(1, 32)
    def _(k):
        pl.semaphore_signal(barrier, inc=1, device_id={"grp": y, "blk": peer(k // 8, lax.rem(k, 8))}, device_id_type=MESH)

    pl.semaphore_wait(barrier, 34)

    def halve(m):
        def step():
            fetch(m).wait()

            @pl.loop(0, 32)
            def _(i):
                hi, lo = split(stage[m % 2, i // 8, lax.rem(i, 8)].reshape(128, 128))
                rows = pl.ds(pl.multiple_of(128 * lax.rem(i, 8), 128), 128)
                halves[4 * m + i // 8, rows, 0:128] = hi
                halves[4 * m + i // 8, rows, 128:256] = lo

            if m + 2 < 8:
                fetch(m + 2).start()
        return step

    gather_coeffs(own, coef, (g1s, g1r, sbs, sbr, one_sem), [halve(m) for m in range(8)])

    @pl.loop(0, 8)
    def _(m):
        a = [aux[4 * m + j] for j in range(4)]
        rank = [sum([((a[i] < a[j]) if i > j else (a[i] <= a[j])).astype(jnp.int32) for i in range(4) if i != j]) for j in range(4)]
        at_rank = [[(rank[i] == j).astype(jnp.int32) for i in range(4)] for j in range(4)]
        tile = [4 * m + sum([at_rank[j][i] * i for i in range(4)]) for j in range(4)]
        level = [sum([at_rank[j][i] * a[i] for i in range(4)]) for j in range(4)]
        for j in range(4):
            e = tile[j]
            ch, cl = split(coef[owner[e], local[e]])
            w = jnp.concatenate([ch, cl], axis=1)
            w = jnp.concatenate([w, w], axis=0)
            for q in range(8):
                p = jnp.dot(halves[e, q * 128:(q + 1) * 128, :], w, preferred_element_type=F32)
                p = p[:, :128] + p[:, 128:]
                if j:
                    p += (level[j] == level[j - 1]).astype(F32) * stage[0, j - 1, q].reshape(128, 128)
                stage[0, j, q] = p.reshape(2, 64, 128)
        mask = dom[m].astype(F32)
        rows = pl.ds(pl.multiple_of(128 * m, 128), 128)
        for v in range(4):
            least = sum([(level[j] < v).astype(jnp.int32) for j in range(4)])
            upto = sum([(level[j] <= v).astype(jnp.int32) for j in range(4)])
            on = mask * (upto > least).astype(F32)
            last = jnp.maximum(upto - 1, 0)
            for q in range(8):
                hi, lo = split(stage[0, last, q].reshape(128, 128) * on)
                cols = pl.ds((v * 8 + q) * 128, 128)
                H[rows, cols] = hi
                L[rows, cols] = lo

    def block(I, J, put):
        ri = pl.ds(I * 256, 256)
        rj = pl.ds(J * 256, 256)
        g = lax.dot_general(H[ri, :], H[rj, :], NT, preferred_element_type=F32)
        g += lax.dot_general(L[ri, :], H[rj, :], NT, preferred_element_type=F32)
        g += lax.dot_general(H[ri, :], L[rj, :], NT, preferred_element_type=F32)
        for u in range(2):
            for v in range(2):
                spot, when = put(u, v)

                def store():
                    for half in range(2):
                        at = u * 128 + half * 64
                        partial[spot, half] = g[at:at + 64, v * 128:(v + 1) * 128]
                if when is None:
                    store()
                elif when is not False:
                    pl.when(when)(store)

    rs = []
    for k, (first, count) in enumerate(CHUNKS):
        @pl.loop(0, 2)
        def _(s):
            if k == 0:
                block(s, 3, lambda u, v: (4 * v + 2 * s + u, None))
            elif k == 1:
                block(2 + s, 3, lambda u, v: (8 + 3 * v + 2 * s + u, s < 1 if (u, v) == (1, 0) else None))
            elif k == 2:
                block(s, 2, lambda u, v: (15 + 4 * v + 2 * s + u, None))
            elif k == 3:
                block(2 - 2 * s, 2 - 2 * s, lambda u, v: (23 + 3 * s + u + v, False if (u, v) == (1, 0) else None))
            else:
                block(s, 1, lambda u, v: (29 + 3 * v + 2 * s + u, s < 1 if (u, v) == (1, 0) else None))

        for d in (1, 3, 2):
            cp = remote(partial.at[pl.ds(first, count), :, pl.ds(16 * plane(d), 16), :], sums.at[d - 1, pl.ds(first, count)],
                        rs_s.at[k, d - 1], rs_r.at[k, d - 1], plane(d), me)
            cp.start()
            rs.append(cp)

    mine = pl.ds(pl.multiple_of(16 * y, 16), 16)
    for k, (first, count) in enumerate(CHUNKS):
        for d in range(3):
            region = sums.at[d, pl.ds(first, count)]
            remote(region, region, rs_s.at[k, d], rs_r.at[k, d], y, me).wait_recv()

        @pl.loop(first, first + count)
        def _(q):
            for half in range(2):
                v = (partial[q, half, mine, :] + sums[0, q, half]) + (sums[1, q, half] + sums[2, q, half])
                if half:
                    both[q, mine, :] = v
                else:
                    take[q] = v

    sends = []

    def start(cp):
        cp.start()
        sends.append(cp)

    def done(region, s, r):
        remote(region, region, s, r, y, me).wait_recv()

    def rows(p, base=0):
        return pl.ds(base + pl.multiple_of(16 * p, 16), 16)

    for i, step in enumerate((1, -1)):
        start(remote(both.at[:, mine, :], both.at[:, mine, :], b_s.at[i], b_r.at[i], plane(step), me))

    @pl.loop(0, 64)
    def _(s):
        placed1[s] = take[pair[s]] * used[s].astype(F32)

    def shipment(src, dst, to, s, r):
        return remote(src, dst, s, r, y, to)

    def ship1(dx, d):
        to = peer(dx, d)
        return remote(placed1.at[pl.ds(2 * to, 2)], got.at[pl.ds(2 * me, 2)], a1_s.at[dx, d], a1_r.at[dx, d], y, to)

    def ship2(dx, d):
        to = peer(dx, d)
        return remote(placed2.at[to // 8, lax.rem(to, 8)], out.at[pl.ds(2 * me, 2), 64:128, :], a2_s.at[dx, d], a2_r.at[dx, d], y, to)

    def sender(dx, d):
        return index(x - dx, z - d // 2 + 4, lax.rem(c + d, 2))

    def each(dx, f):
        @pl.loop(1 if dx == 0 else 0, 8)
        def _(d):
            f(dx, d)

    order = (0, 1, 3, 2)
    for dx in order:
        each(dx, lambda dx, d: ship1(dx, d).start())
    own1 = pltpu.make_async_copy(placed1.at[pl.ds(2 * me, 2)], got.at[pl.ds(2 * me, 2)], loc.at[4])
    own1.start()
    for i, step in enumerate((1, -1)):
        done(both.at[:, rows(plane(-step)), :], b_s.at[i], b_r.at[i])
        region = both.at[pl.ds(18 * i, 18), rows(plane(-step)), :]
        start(remote(region, region, b_s.at[2 + i], b_r.at[2 + i], plane(step), me))
    own1.wait()
    locals_ = []
    for dx in order:
        each(dx, lambda dx, d: done(got.at[pl.ds(2 * sender(dx, d), 2)], a1_s.at[dx, d], a1_r.at[dx, d]))
        first = 16 * lax.rem(x - dx + 4, 4)
        for i, step in enumerate((1, -1)):
            start(remote(got.at[pl.ds(first, 16)], out.at[pl.ds(first, 16), rows(y), :], w_s.at[dx, i], w_r.at[dx, i], plane(step), me))
        cp = pltpu.make_async_copy(got.at[pl.ds(first, 16)], out.at[pl.ds(first, 16), rows(y), :], loc.at[dx])
        cp.start()
        locals_.append(cp)
    for i in range(2):
        done(both.at[pl.ds(18 * i, 18), rows(plane(2)), :], b_s.at[2 + i], b_r.at[2 + i])

    @pl.loop(0, 64)
    def _(s):
        placed2[s // 16, lax.rem(s // 2, 8), lax.rem(s, 2)] = both[pair[s]] * used[s].astype(F32)

    for dx in (1, 3, 2, 0):
        each(dx, lambda dx, d: ship2(dx, d).start())
    cp = pltpu.make_async_copy(placed2.at[me // 8, lax.rem(me, 8)], out.at[pl.ds(2 * me, 2), 64:128, :], loc.at[5])
    cp.start()
    locals_.append(cp)
    for dx in order:
        first = 16 * lax.rem(x - dx + 4, 4)
        for i, step in enumerate((1, -1)):
            done(out.at[pl.ds(first, 16), rows(plane(-step)), :], w_s.at[dx, i], w_r.at[dx, i])
            region = out.at[pl.ds(first + 8 * i, 8), rows(plane(-step)), :]
            start(remote(region, region, w_s.at[dx, 2 + i], w_r.at[dx, 2 + i], plane(step), me))
    for dx in order:
        first = 16 * lax.rem(x - dx + 4, 4)
        for i in range(2):
            done(out.at[pl.ds(first + 8 * i, 8), rows(plane(2)), :], w_s.at[dx, 2 + i], w_r.at[dx, 2 + i])
    for dx in order:
        each(dx, lambda dx, d: done(out.at[pl.ds(2 * sender(dx, d), 2), 64:128, :], a2_s.at[dx, d], a2_r.at[dx, d]))
    for cp in locals_:
        cp.wait()
    for cp in rs + sends:
        cp.wait_send()
    for dx in range(4):
        each(dx, lambda dx, d: ship1(dx, d).wait_send())
        each(dx, lambda dx, d: ship2(dx, d).wait_send())


def fused(tiles, coeffs, domains, owner, local, aux, pair, used):
    vm = pl.BlockSpec(memory_space=pltpu.VMEM)
    sm = pl.BlockSpec(memory_space=pltpu.SMEM)
    hbm = pl.BlockSpec(memory_space=pl.ANY)
    dma = pltpu.SemaphoreType.DMA
    return pl.pallas_call(
        body,
        out_shape=jax.ShapeDtypeStruct((64, 128, 128), F32),
        in_specs=[hbm, hbm, sm, sm, sm, vm, sm, sm],
        out_specs=hbm,
        scratch_shapes=[
            pltpu.VMEM((32, 8, 128, 128), F32), pltpu.VMEM((32, 1024, 256), BF16), pltpu.VMEM((2, 4, 8, 2, 64, 128), F32),
            pltpu.VMEM((1024, 4096), BF16), pltpu.VMEM((1024, 4096), BF16),
            pltpu.VMEM((36, 2, 64, 128), F32), pltpu.VMEM((3, 36, 2, 16, 128), F32), pltpu.VMEM((36, 16, 128), F32),
            pltpu.VMEM((36, 64, 128), F32), pltpu.VMEM((64, 16, 128), F32), pltpu.VMEM((64, 16, 128), F32),
            dma((44,)), dma((44,)), dma((45,)), dma((45,)), dma, dma((8,)), dma((5, 3)), dma((5, 3)), dma((4,)), dma((4,)),
            dma((4, 8)), dma((4, 8)), dma((4, 8)), dma((4, 8)), dma((4, 4)), dma((4, 4)), dma((6,))],
        compiler_params=pltpu.CompilerParams(collective_id=1, has_side_effects=True, vmem_limit_bytes=63 * 2**20),
        cost_estimate=pl.CostEstimate(flops=2 * 10**10, bytes_accessed=22 * 10**6, transcendentals=0),
    )(coeffs.reshape(8, 128, 128), tiles.reshape(32, 8, 2, 64, 128), owner, local, aux, domains.reshape(8, 1, 128), pair, used)


def pair_rank(owner):
    at = jnp.arange(owner.shape[0])
    same = (owner[:, None] == owner[None, :]) & (at[None, :] < at[:, None])
    return jnp.sum(same.astype(jnp.int32), axis=1)


def on_device(tiles, coeffs, domains, tile_owner, tile_local, tile_aux, pair_owner):
    targets = pair_owner[:, 0]
    slot = targets * 2 + pair_rank(targets)
    placing = (jnp.arange(64)[:, None] == slot[None, :]).astype(jnp.int32)
    used = jnp.sum(placing, axis=1)
    pair = jnp.sum(placing * jnp.asarray(places())[None, :], axis=1)
    return fused(tiles, coeffs, domains, tile_owner[:, 0], tile_local, tile_aux, pair, used)


def solution(mesh):
    placed = (
        P(("grp", "blk"), None, None, None),
        P("blk", None),
        P("blk", None),
        P(("grp", "blk"), None),
        P(("grp", "blk")),
        P(("grp", "blk")),
        P("blk", None),
    )
    return jax.shard_map(
        on_device, mesh=mesh, in_specs=placed, out_specs=P("blk", None, None), check_vma=False
    )
```

time: 387 us -> 149 us (0.39)
  waiting for transfers between devices: 166 us -> 0 us
  Pallas kernels: 0 us -> 141 us
  matrix products: 96.3 us -> 0 us
  blocking collectives: 55.8 us -> 0 us
  local copies, waits for them, and re-layouts: 51.1 us -> 4.7 us
  between operations: 13.4 us -> 0.01 us
    pallas_call x0 -> x1, Pallas kernels: none -> 141 us  [fused(): pl.pallas_call(body, out_shape=jax.ShapeDtypeStruct((64, 128, 128), F32),...]
    dot_general x4 -> x0, matrix products: 96.3 us -> none  [the longest x1 56.2 us: on_device(): gram = jnp.einsum('aprj,bpsj->abrs', factors, factors, precision=HIGH)]
    psum x1 -> x0, waiting for transfers between devices: 90.5 us -> none  [on_device(): received = lax.psum(received, 'grp')]
    all_gather x1 -> x0, waiting for transfers between devices: 75 us -> none  [on_device(): gathered = lax.all_gather(coeffs, 'blk', axis=0, tiled=True)]
    all_to_all x1 -> x0, blocking collectives: 55.8 us -> none  [on_device(): lax.all_to_all(outgoing, 'blk', split_axis=0, concat_axis=0, tiled=True)]
    dot_general x2 -> x0, local copies, waits for them, and re-layouts: 26.8 us -> none  [the longest x1 17.4 us: on_device(): products = jnp.einsum('eprs,esj->eprj', tiles, picked, precision=HIGH)]
    gather x2 -> x0, local copies, waits for them, and re-layouts: 9.36 us -> none  [the longest x1 6.45 us: on_device(): picked = gathered[source]]
    transpose x1 -> x0, local copies, waits for them, and re-layouts: 5.36 us -> none  [on_device(): gram = jnp.einsum('aprj,bpsj->abrs', factors, factors, precision=HIGH)]
  transfers between devices with their start and end apart: 2 -> 0, of which waited for: 2 -> 0; matrix products, arithmetic and copies ran while one was open for 1% -> 0% of each run, Pallas kernels for 0% -> 0%
where the time goes in v3:
time: 149 us; the launch traced here: 148 us
  Pallas kernels  141 us (95%)
  local copies, waits for them, and re-layouts  4.7 us (3%)
  other arithmetic  2.84 us (2%)
    pallas_call x1, Pallas kernels, fused(): pl.pallas_call(body, out_shape=jax.ShapeDtypeStruct((64, 128, 128), F32),...  141 us
    unnamed x1, local copies, waits for them, and re-layouts  4.7 us

profile of v3, /device:TPU:1, one launch (start us, length us, event | category | flops | bytes accessed | tf_op | source)
XLA Modules:
  0.0 148.4 jit_solution(7291448558255180715)
XLA Ops:
  0.0 0.9 convert_reduce_fusion.1
  0.9 0.7 multiply_add_fusion
  1.6 1.3 convert_reduce_fusion
  2.8 140.8 %shard_map.82 = f32[64,128,128]{2,1,0:T(8,128)} custom-call(f32[8,128,128]{2,1,0:T(8,128)} %bitcast.7, f32[32,8,2,64,128]{4,3,2,1,0:T(8,128)} %bitcast.6, s32[32]{0:T(128)} %bitcast.10, s32[32]{0:T(128)} %local.1, s32[32]{0:T(128)} %aux.1, s32[8,1,128]{2,1,0:T(1,128)} %bitcast.8, s32[64]{0:T(128)} %get-tuple-element.6.pair, s32[64]{0:T(128)} %get-tuple-element.5.used), custom_call_target="tpu_custom_call" | custom-call | flops 20000000000 | bytes 22000000 | tf_op jit(solution)/shard_map/pallas_call | solution.py:389
  143.7 4.7 %copy.10 = f32[64,128,128]{2,1,0:T(8,128)} copy(f32[64,128,128]{2,1,0:T(8,128)} %shard_map.82) | data formatting | bytes 8388608

commit v4 on v3

--- a/solution.py
+++ b/solution.py
@@ -9,6 +9,7 @@
 F32, BF16 = jnp.float32, jnp.bfloat16
 MESH = pl.DeviceIdType.MESH
 NT = (((1,), (1,)), ((), ()))
+QUARTERED = ("0",)
 CHUNKS = ((0, 8), (8, 7), (15, 8), (23, 6), (29, 7))
 
 
@@ -45,7 +46,7 @@
 
 
 def gather_coeffs(own, coef, sems, work):
-    send, recv, sib_send, sib_recv, local_sem = sems
+    send, recv, sib_send, sib_recv, y_send, y_recv, local_sem = sems
     x, y, z, c = coords()
     me = index(x, z, c)
     other = index(x, z, 1 - c)
@@ -73,7 +74,13 @@
     table = {}
 
     def define(part, key, du, dv, lo, n):
-        table[part, key] = (len(table), du, dv, part * 4 + lo, n)
+        quarter = key[0] in ("v", "vv") and key[2] in QUARTERED
+        if not quarter:
+            table[part, key] = (len(table), du, dv, lambda ref: ref.at[pl.ds(part * 4 + lo, n)], (part * 4 + lo, n))
+        elif key[0] == "v":
+            table[part, key] = (len(table), du, dv, lambda ref: ref.at[part * 4 + y], None)
+        else:
+            table[part, key] = (len(table), du, dv, lambda ref: ref.at[part * 4 + y, pl.ds(32 * lo, 64)], None)
 
     for part in range(2):
         define(part, "u+", -1, 0, 0, 4)
@@ -87,18 +94,57 @@
                 define(part, ("vv", sign, name), du, -2 * sign, 0 if sign > 0 else 2, 2)
 
     def post(part, key, du_to, dv_to, src=None):
-        k, du, dv, lo, n = table[part, key]
-        region = coef.at[at(part, du + du_to, dv + dv_to), pl.ds(lo, n)]
-        cp = remote(region if src is None else src.at[pl.ds(lo, n)], region, at(part, du_to, dv_to), send.at[k], recv.at[k])
+        k, du, dv, blocks, share = table[part, key]
+        region = blocks(coef.at[at(part, du + du_to, dv + dv_to)])
+        cp = remote(region if src is None else blocks(src), region, at(part, du_to, dv_to), send.at[k], recv.at[k])
         cp.start()
         sends.append(cp)
 
     def arrive(part, key):
-        k, du, dv, lo, n = table[part, key]
+        k, du, dv, blocks, share = table[part, key]
         source = at(part, du, dv)
-        region = coef.at[source, pl.ds(lo, n)]
+        region = blocks(coef.at[source])
         remote(region, region, me, send.at[k], recv.at[k]).wait_recv()
-        sibling(source, lo, n)
+        if share:
+            sibling(source, *share)
+
+    def plane(d):
+        return lax.rem(y + d + 4, 4)
+
+    def swap(part, name, dv, i, block, half, to, sem):
+        source = at(part, {"0": 0, "m": -1}[name], dv)
+        k = (part * len(QUARTERED) + QUARTERED.index(name)) * 3 + dv % 4 - 1
+        region = coef.at[source, part * 4 + block]
+        if half:
+            region = region.at[pl.ds(64 * i, 64)]
+        return pltpu.make_async_remote_copy(src_ref=region, dst_ref=region, send_sem=y_send.at[k, sem], recv_sem=y_recv.at[k, sem],
+                                            device_id={"grp": to, "blk": me}, device_id_type=MESH)
+
+    def swap_start(name, dv):
+        for part in range(2):
+            for i, step in enumerate((1, -1)):
+                cp = swap(part, name, dv, i, y, False, plane(step), i)
+                cp.start()
+                sends.append(cp)
+
+    def swap_on(name, dv):
+        for part in range(2):
+            for i, step in enumerate((1, -1)):
+                swap(part, name, dv, i, plane(-step), False, y, i).wait_recv()
+                cp = swap(part, name, dv, i, plane(-step), True, plane(step), 2 + i)
+                cp.start()
+                sends.append(cp)
+
+    def swap_end(name, dv):
+        for part in range(2):
+            for i in range(2):
+                swap(part, name, dv, i, plane(2), True, y, 2 + i).wait_recv()
+            sibling(at(part, {"0": 0, "m": -1}[name], dv), part * 4, 4)
+
+    def quartered(name, f, *dvs):
+        if name in QUARTERED:
+            for dv in dvs:
+                f(name, dv)
 
     def meanwhile():
         if work:
@@ -124,6 +170,7 @@
         for part in range(2):
             arrive(part, ("v", sign, "0"))
             post(part, ("vv", sign, "0"), 0, sign)
+    quartered("0", swap_start, 1, -1)
     meanwhile()
     for key, name in (("uu+", "2l"), ("uu-", "2h")):
         for part in range(2):
@@ -131,12 +178,29 @@
             post(part, ("v", 1, name), 0, 1)
             post(part, ("v", -1, name), 0, -1)
     meanwhile()
-    for name in ("m", "p"):
-        for sign in (1, -1):
-            for part in range(2):
-                arrive(part, ("v", sign, name))
-                post(part, ("vv", sign, name), 0, sign)
-        meanwhile()
+    for sign in (1, -1):
+        for part in range(2):
+            arrive(part, ("v", sign, "m"))
+            post(part, ("vv", sign, "m"), 0, sign)
+    quartered("m", swap_start, 1, -1)
+    meanwhile()
+    for sign in (1, -1):
+        for part in range(2):
+            arrive(part, ("vv", sign, "0"))
+    quartered("0", swap_start, 2)
+    quartered("0", swap_on, 1, -1)
+    for sign in (1, -1):
+        for part in range(2):
+            arrive(part, ("v", sign, "p"))
+            post(part, ("vv", sign, "p"), 0, sign)
+    meanwhile()
+    for sign in (1, -1):
+        for part in range(2):
+            arrive(part, ("vv", sign, "m"))
+    quartered("m", swap_start, 2)
+    quartered("0", swap_end, 1, -1)
+    quartered("0", swap_on, 2)
+    quartered("m", swap_on, 1, -1)
     for sign, name, drop in ((1, "2l", "2h"), (-1, "2h", "2l")):
         for part in range(2):
             arrive(part, ("v", sign, name))
@@ -144,10 +208,14 @@
             arrive(part, ("v", -sign, name))
     while work:
         meanwhile()
-    for name in ("0", "m", "p", "2"):
+    quartered("m", swap_on, 2)
+    quartered("0", swap_end, 2)
+    quartered("m", swap_end, 1, -1)
+    for name in ("p", "2"):
         for sign in (1, -1):
             for part in range(2):
                 arrive(part, ("vv", sign, name))
+    quartered("m", swap_end, 2)
     here.wait()
     for k, (source, lo, n, cp) in enumerate(sibs):
         region = coef.at[source + 1 - 2 * c, pl.ds(lo, n)]
@@ -156,9 +224,9 @@
         cp.wait_send()
 
 
-def body(own, tiles, owner, local, aux, dom, pair, used, out,
+def body(own, tiles, owner, local, aux, dom, first_pair, last_pair, out,
          coef, halves, stage, H, L, partial, sums, take, both, placed1, got,
-         g1s, g1r, sbs, sbr, one_sem, st_sem, rs_s, rs_r, b_s, b_r, a1_s, a1_r, a2_s, a2_r, w_s, w_r, loc):
+         g1s, g1r, sbs, sbr, ys, yr, one_sem, st_sem, rs_s, rs_r, b_s, b_r, a1_s, a1_r, a2_s, a2_r, w_s, w_r, loc):
     placed2 = stage.at[1]
     x, y, z, c = coords()
     me = index(x, z, c)
@@ -179,14 +247,10 @@
     fetch(0).start()
     fetch(1).start()
     barrier = pltpu.get_barrier_semaphore()
-    for d in (1, 2, 3):
-        pl.semaphore_signal(barrier, inc=1, device_id={"grp": plane(d), "blk": me}, device_id_type=MESH)
-
-    @pl.loop(1, 32)
-    def _(k):
-        pl.semaphore_signal(barrier, inc=1, device_id={"grp": y, "blk": peer(k // 8, lax.rem(k, 8))}, device_id_type=MESH)
-
-    pl.semaphore_wait(barrier, 34)
+    for g, b in ((plane(1), me), (plane(-1), me), (plane(2), me), (y, index(x, z, 1 - c)), (y, index(x + 1, z, c)),
+                 (y, index(x - 1, z, c)), (y, index(x, z + 1, c)), (y, index(x, z - 1, c))):
+        pl.semaphore_signal(barrier, inc=1, device_id={"grp": g, "blk": b}, device_id_type=MESH)
+    pl.semaphore_wait(barrier, 8)
 
     def halve(m):
         def step():
@@ -203,7 +267,7 @@
                 fetch(m + 2).start()
         return step
 
-    gather_coeffs(own, coef, (g1s, g1r, sbs, sbr, one_sem), [halve(m) for m in range(8)])
+    gather_coeffs(own, coef, (g1s, g1r, sbs, sbr, ys, yr, one_sem), [halve(m) for m in range(8)])
 
     @pl.loop(0, 8)
     def _(m):
@@ -306,9 +370,17 @@
     for i, step in enumerate((1, -1)):
         start(remote(both.at[:, mine, :], both.at[:, mine, :], b_s.at[i], b_r.at[i], plane(step), me))
 
+    def slot(s):
+        o = s // 2
+        second = lax.rem(s, 2)
+        early, late = first_pair[o], last_pair[o]
+        spot = lax.rem(jnp.maximum(jnp.where(second == 1, late, early), 0), 64)
+        return spot, jnp.where(second == 1, late > early, early < 4096).astype(F32)
+
     @pl.loop(0, 64)
     def _(s):
-        placed1[s] = take[pair[s]] * used[s].astype(F32)
+        spot, filled = slot(s)
+        placed1[s] = take[spot] * filled
 
     def shipment(src, dst, to, s, r):
         return remote(src, dst, s, r, y, to)
@@ -353,7 +425,8 @@
 
     @pl.loop(0, 64)
     def _(s):
-        placed2[s // 16, lax.rem(s // 2, 8), lax.rem(s, 2)] = both[pair[s]] * used[s].astype(F32)
+        spot, filled = slot(s)
+        placed2[s // 16, lax.rem(s // 2, 8), lax.rem(s, 2)] = both[spot] * filled
 
     for dx in (1, 3, 2, 0):
         each(dx, lambda dx, d: ship2(dx, d).start())
@@ -381,7 +454,7 @@
         each(dx, lambda dx, d: ship2(dx, d).wait_send())
 
 
-def fused(tiles, coeffs, domains, owner, local, aux, pair, used):
+def fused(tiles, coeffs, domains, owner, local, aux, first_pair, last_pair):
     vm = pl.BlockSpec(memory_space=pltpu.VMEM)
     sm = pl.BlockSpec(memory_space=pltpu.SMEM)
     hbm = pl.BlockSpec(memory_space=pl.ANY)
@@ -396,26 +469,20 @@
             pltpu.VMEM((1024, 4096), BF16), pltpu.VMEM((1024, 4096), BF16),
             pltpu.VMEM((36, 2, 64, 128), F32), pltpu.VMEM((3, 36, 2, 16, 128), F32), pltpu.VMEM((36, 16, 128), F32),
             pltpu.VMEM((36, 64, 128), F32), pltpu.VMEM((64, 16, 128), F32), pltpu.VMEM((64, 16, 128), F32),
-            dma((44,)), dma((44,)), dma((45,)), dma((45,)), dma, dma((8,)), dma((5, 3)), dma((5, 3)), dma((4,)), dma((4,)),
+            dma((44,)), dma((44,)), dma((45,)), dma((45,)), dma((6 * len(QUARTERED), 4)), dma((6 * len(QUARTERED), 4)), dma,
+            dma((8,)), dma((5, 3)), dma((5, 3)), dma((4,)), dma((4,)),
             dma((4, 8)), dma((4, 8)), dma((4, 8)), dma((4, 8)), dma((4, 4)), dma((4, 4)), dma((6,))],
         compiler_params=pltpu.CompilerParams(collective_id=1, has_side_effects=True, vmem_limit_bytes=63 * 2**20),
         cost_estimate=pl.CostEstimate(flops=2 * 10**10, bytes_accessed=22 * 10**6, transcendentals=0),
-    )(coeffs.reshape(8, 128, 128), tiles.reshape(32, 8, 2, 64, 128), owner, local, aux, domains.reshape(8, 1, 128), pair, used)
-
-
-def pair_rank(owner):
-    at = jnp.arange(owner.shape[0])
-    same = (owner[:, None] == owner[None, :]) & (at[None, :] < at[:, None])
-    return jnp.sum(same.astype(jnp.int32), axis=1)
+    )(coeffs.reshape(8, 128, 128), tiles.reshape(32, 8, 2, 64, 128), owner, local, aux, domains.reshape(8, 1, 128), first_pair, last_pair)
 
 
 def on_device(tiles, coeffs, domains, tile_owner, tile_local, tile_aux, pair_owner):
-    targets = pair_owner[:, 0]
-    slot = targets * 2 + pair_rank(targets)
-    placing = (jnp.arange(64)[:, None] == slot[None, :]).astype(jnp.int32)
-    used = jnp.sum(placing, axis=1)
-    pair = jnp.sum(placing * jnp.asarray(places())[None, :], axis=1)
-    return fused(tiles, coeffs, domains, tile_owner[:, 0], tile_local, tile_aux, pair, used)
+    named = pair_owner[:, 0][None, :] == jnp.arange(32)[:, None]
+    code = jnp.asarray(np.arange(36, dtype=np.int32) * 64 + places())[None, :]
+    first_pair = jnp.min(jnp.where(named, code, 4096), axis=1)
+    last_pair = jnp.max(jnp.where(named, code, -1), axis=1)
+    return fused(tiles, coeffs, domains, tile_owner[:, 0], tile_local, tile_aux, first_pair, last_pair)
 
 
 def solution(mesh):

time: 149 us -> 141 us (0.946)
  Pallas kernels: 141 us -> 135 us
  other arithmetic: 2.84 us -> 1.31 us
    pallas_call x1, Pallas kernels: 141 us -> 135 us  [fused(): pl.pallas_call(body, out_shape=jax.ShapeDtypeStruct((64, 128, 128), F32),...]
    reduce_sum x2 -> x0, other arithmetic: 2.18 us -> none  [the longest x1 1.27 us: on_device(): used = jnp.sum(placing, axis=1)]
where the time goes in v4:
time: 141 us
  Pallas kernels  135 us (96%)
  local copies, waits for them, and re-layouts  4.7 us (3%)
    pallas_call x1, Pallas kernels, fused(): pl.pallas_call(body, out_shape=jax.ShapeDtypeStruct((64, 128, 128), F32),...  135 us
    unnamed x1, local copies, waits for them, and re-layouts  4.7 us

profile of v4, /device:TPU:1, one launch (start us, length us, event | category | flops | bytes accessed | tf_op | source)
XLA Modules:
  0.0 141.4 jit_solution(5254373767374331448)
XLA Ops:
  0.0 1.3 select_reduce_fusion
  1.3 135.3 %shard_map.82 = f32[64,128,128]{2,1,0:T(8,128)} custom-call(f32[8,128,128]{2,1,0:T(8,128)} %bitcast.7, f32[32,8,2,64,128]{4,3,2,1,0:T(8,128)} %bitcast.6, s32[32]{0:T(128)} %bitcast.9, s32[32]{0:T(128)} %local.1, s32[32]{0:T(128)} %aux.1, s32[8,1,128]{2,1,0:T(1,128)} %bitcast.8, s32[32]{0:T(128)} %get-tuple-element.6.first_pair, s32[32]{0:T(128)} %get-tuple-element.5.last_pair), custom_call_target="tpu_custom_call" | custom-call | flops 20000000000 | bytes 22000000 | tf_op jit(solution)/shard_map/pallas_call | solution.py:462
  136.7 4.7 %copy.10 = f32[64,128,128]{2,1,0:T(8,128)} copy(f32[64,128,128]{2,1,0:T(8,128)} %shard_map.82) | data formatting | bytes 8388608

commit v5 on v4

--- a/solution.py
+++ b/solution.py
@@ -225,9 +225,10 @@
 
 
 def body(own, tiles, owner, local, aux, dom, first_pair, last_pair, out,
-         coef, halves, stage, H, L, partial, sums, take, both, placed1, got,
+         coef, halves, stage, H, L, partial, sums, take, both0, both1, placed1, got,
          g1s, g1r, sbs, sbr, ys, yr, one_sem, st_sem, rs_s, rs_r, b_s, b_r, a1_s, a1_r, a2_s, a2_r, w_s, w_r, loc):
     placed2 = stage.at[1]
+    both = both0, both1
     x, y, z, c = coords()
     me = index(x, z, c)
 
@@ -311,9 +312,12 @@
                 spot, when = put(u, v)
 
                 def store():
-                    for half in range(2):
-                        at = u * 128 + half * 64
-                        partial[spot, half] = g[at:at + 64, v * 128:(v + 1) * 128]
+                    cols = slice(v * 128, (v + 1) * 128)
+                    partial[spot, 0] = g[u * 128:u * 128 + 64, cols]
+                    for p in range(4):
+                        for t in range(2):
+                            at = u * 128 + 64 + 32 * t + 8 * p
+                            partial[spot, 1, 16 * p + 8 * t:16 * p + 8 * t + 8, :] = g[at:at + 8, cols]
                 if when is None:
                     store()
                 elif when is not False:
@@ -351,7 +355,8 @@
             for half in range(2):
                 v = (partial[q, half, mine, :] + sums[0, q, half]) + (sums[1, q, half] + sums[2, q, half])
                 if half:
-                    both[q, mine, :] = v
+                    both[0][y, q] = v[0:8]
+                    both[1][y, q] = v[8:16]
                 else:
                     take[q] = v
 
@@ -367,8 +372,9 @@
     def rows(p, base=0):
         return pl.ds(base + pl.multiple_of(16 * p, 16), 16)
 
-    for i, step in enumerate((1, -1)):
-        start(remote(both.at[:, mine, :], both.at[:, mine, :], b_s.at[i], b_r.at[i], plane(step), me))
+    for t in range(2):
+        for i, step in enumerate((1, -1)):
+            start(remote(both[t].at[y], both[t].at[y], b_s.at[t, i], b_r.at[t, i], plane(step), me))
 
     def slot(s):
         o = s // 2
@@ -389,9 +395,10 @@
         to = peer(dx, d)
         return remote(placed1.at[pl.ds(2 * to, 2)], got.at[pl.ds(2 * me, 2)], a1_s.at[dx, d], a1_r.at[dx, d], y, to)
 
-    def ship2(dx, d):
+    def ship2(t, dx, d):
         to = peer(dx, d)
-        return remote(placed2.at[to // 8, lax.rem(to, 8)], out.at[pl.ds(2 * me, 2), 64:128, :], a2_s.at[dx, d], a2_r.at[dx, d], y, to)
+        return remote(placed2.at[to // 8, lax.rem(to, 8), :, pl.ds(32 * t, 32)], out.at[pl.ds(2 * me, 2), pl.ds(64 + 32 * t, 32), :],
+                      a2_s.at[t, dx, d], a2_r.at[t, dx, d], y, to)
 
     def sender(dx, d):
         return index(x - dx, z - d // 2 + 4, lax.rem(c + d, 2))
@@ -406,12 +413,33 @@
         each(dx, lambda dx, d: ship1(dx, d).start())
     own1 = pltpu.make_async_copy(placed1.at[pl.ds(2 * me, 2)], got.at[pl.ds(2 * me, 2)], loc.at[4])
     own1.start()
-    for i, step in enumerate((1, -1)):
-        done(both.at[:, rows(plane(-step)), :], b_s.at[i], b_r.at[i])
-        region = both.at[pl.ds(18 * i, 18), rows(plane(-step)), :]
-        start(remote(region, region, b_s.at[2 + i], b_r.at[2 + i], plane(step), me))
+    for t in range(2):
+        for i, step in enumerate((1, -1)):
+            done(both[t].at[plane(-step)], b_s.at[t, i], b_r.at[t, i])
+            region = both[t].at[plane(-step), pl.ds(18 * i, 18)]
+            start(remote(region, region, b_s.at[t, 2 + i], b_r.at[t, 2 + i], plane(step), me))
+    locals_ = []
+
+    def ship_whole(t):
+        for i in range(2):
+            done(both[t].at[plane(2), pl.ds(18 * i, 18)], b_s.at[t, 2 + i], b_r.at[t, 2 + i])
+
+        @pl.loop(0, 64)
+        def _(s):
+            spot, filled = slot(s)
+            for p in range(4):
+                at = 32 * t + 8 * p
+                placed2[s // 16, lax.rem(s // 2, 8), lax.rem(s, 2), at:at + 8, :] = both[t][p, spot] * filled
+
+        for dx in (1, 3, 2, 0):
+            each(dx, lambda dx, d: ship2(t, dx, d).start())
+        cp = pltpu.make_async_copy(placed2.at[me // 8, lax.rem(me, 8), :, pl.ds(32 * t, 32)],
+                                   out.at[pl.ds(2 * me, 2), pl.ds(64 + 32 * t, 32), :], loc.at[5 + t])
+        cp.start()
+        locals_.append(cp)
+
+    ship_whole(0)
     own1.wait()
-    locals_ = []
     for dx in order:
         each(dx, lambda dx, d: done(got.at[pl.ds(2 * sender(dx, d), 2)], a1_s.at[dx, d], a1_r.at[dx, d]))
         first = 16 * lax.rem(x - dx + 4, 4)
@@ -420,19 +448,7 @@
         cp = pltpu.make_async_copy(got.at[pl.ds(first, 16)], out.at[pl.ds(first, 16), rows(y), :], loc.at[dx])
         cp.start()
         locals_.append(cp)
-    for i in range(2):
-        done(both.at[pl.ds(18 * i, 18), rows(plane(2)), :], b_s.at[2 + i], b_r.at[2 + i])
-
-    @pl.loop(0, 64)
-    def _(s):
-        spot, filled = slot(s)
-        placed2[s // 16, lax.rem(s // 2, 8), lax.rem(s, 2)] = both[spot] * filled
-
-    for dx in (1, 3, 2, 0):
-        each(dx, lambda dx, d: ship2(dx, d).start())
-    cp = pltpu.make_async_copy(placed2.at[me // 8, lax.rem(me, 8)], out.at[pl.ds(2 * me, 2), 64:128, :], loc.at[5])
-    cp.start()
-    locals_.append(cp)
+    ship_whole(1)
     for dx in order:
         first = 16 * lax.rem(x - dx + 4, 4)
         for i, step in enumerate((1, -1)):
@@ -443,15 +459,18 @@
         first = 16 * lax.rem(x - dx + 4, 4)
         for i in range(2):
             done(out.at[pl.ds(first + 8 * i, 8), rows(plane(2)), :], w_s.at[dx, 2 + i], w_r.at[dx, 2 + i])
-    for dx in order:
-        each(dx, lambda dx, d: done(out.at[pl.ds(2 * sender(dx, d), 2), 64:128, :], a2_s.at[dx, d], a2_r.at[dx, d]))
+    for t in range(2):
+        for dx in order:
+            each(dx, lambda dx, d: done(out.at[pl.ds(2 * sender(dx, d), 2), pl.ds(64 + 32 * t, 32), :], a2_s.at[t, dx, d],
+                                        a2_r.at[t, dx, d]))
     for cp in locals_:
         cp.wait()
     for cp in rs + sends:
         cp.wait_send()
     for dx in range(4):
         each(dx, lambda dx, d: ship1(dx, d).wait_send())
-        each(dx, lambda dx, d: ship2(dx, d).wait_send())
+        for t in range(2):
+            each(dx, lambda dx, d: ship2(t, dx, d).wait_send())
 
 
 def fused(tiles, coeffs, domains, owner, local, aux, first_pair, last_pair):
@@ -468,13 +487,33 @@
             pltpu.VMEM((32, 8, 128, 128), F32), pltpu.VMEM((32, 1024, 256), BF16), pltpu.VMEM((2, 4, 8, 2, 64, 128), F32),
             pltpu.VMEM((1024, 4096), BF16), pltpu.VMEM((1024, 4096), BF16),
             pltpu.VMEM((36, 2, 64, 128), F32), pltpu.VMEM((3, 36, 2, 16, 128), F32), pltpu.VMEM((36, 16, 128), F32),
-            pltpu.VMEM((36, 64, 128), F32), pltpu.VMEM((64, 16, 128), F32), pltpu.VMEM((64, 16, 128), F32),
+            pltpu.VMEM((4, 36, 8, 128), F32), pltpu.VMEM((4, 36, 8, 128), F32), pltpu.VMEM((64, 16, 128), F32), pltpu.VMEM((64, 16, 128), F32),
             dma((44,)), dma((44,)), dma((45,)), dma((45,)), dma((6 * len(QUARTERED), 4)), dma((6 * len(QUARTERED), 4)), dma,
-            dma((8,)), dma((5, 3)), dma((5, 3)), dma((4,)), dma((4,)),
-            dma((4, 8)), dma((4, 8)), dma((4, 8)), dma((4, 8)), dma((4, 4)), dma((4, 4)), dma((6,))],
+            dma((8,)), dma((5, 3)), dma((5, 3)), dma((2, 4)), dma((2, 4)),
+            dma((4, 8)), dma((4, 8)), dma((2, 4, 8)), dma((2, 4, 8)), dma((4, 4)), dma((4, 4)), dma((7,))],
         compiler_params=pltpu.CompilerParams(collective_id=1, has_side_effects=True, vmem_limit_bytes=63 * 2**20),
         cost_estimate=pl.CostEstimate(flops=2 * 10**10, bytes_accessed=22 * 10**6, transcendentals=0),
     )(coeffs.reshape(8, 128, 128), tiles.reshape(32, 8, 2, 64, 128), owner, local, aux, domains.reshape(8, 1, 128), first_pair, last_pair)
+
+
+def copy_body(src, dst, held, into, out_of):
+    arrive = [pltpu.make_async_copy(src.at[pl.ds(8 * i, 8)], held.at[pl.ds(8 * i, 8)], into.at[i]) for i in range(8)]
+    leave = [pltpu.make_async_copy(held.at[pl.ds(8 * i, 8)], dst.at[pl.ds(8 * i, 8)], out_of.at[i]) for i in range(8)]
+    for cp in arrive:
+        cp.start()
+    for a, b in zip(arrive, leave):
+        a.wait()
+        b.start()
+    for cp in leave:
+        cp.wait()
+
+
+def copied(value):
+    hbm = pl.BlockSpec(memory_space=pl.ANY)
+    return pl.pallas_call(
+        copy_body, in_specs=[hbm], out_specs=hbm, out_shape=jax.ShapeDtypeStruct((64, 128, 128), F32),
+        scratch_shapes=[pltpu.VMEM((64, 128, 128), F32), pltpu.SemaphoreType.DMA((8,)), pltpu.SemaphoreType.DMA((8,))],
+        compiler_params=pltpu.CompilerParams(vmem_limit_bytes=60 * 2**20))(value)
 
 
 def on_device(tiles, coeffs, domains, tile_owner, tile_local, tile_aux, pair_owner):
@@ -482,7 +521,7 @@
     code = jnp.asarray(np.arange(36, dtype=np.int32) * 64 + places())[None, :]
     first_pair = jnp.min(jnp.where(named, code, 4096), axis=1)
     last_pair = jnp.max(jnp.where(named, code, -1), axis=1)
-    return fused(tiles, coeffs, domains, tile_owner[:, 0], tile_local, tile_aux, first_pair, last_pair)
+    return copied(fused(tiles, coeffs, domains, tile_owner[:, 0], tile_local, tile_aux, first_pair, last_pair))
 
 
 def solution(mesh):

time: 141 us -> 139 us (0.986)
  local copies, waits for them, and re-layouts: 4.7 us -> 0 us
  Pallas kernels: 135 us -> 138 us
    unnamed x1 -> x0, local copies, waits for them, and re-layouts: 4.7 us -> none
    pallas_call x0 -> x1, Pallas kernels: none -> 3.58 us  [copied(): pl.pallas_call(copy_body, in_specs=[hbm], out_specs=hbm, out_shape=jax.Sh...]
where the time goes in v5:
time: 139 us
  Pallas kernels  138 us (99%)
    pallas_call x1, Pallas kernels, fused(): pl.pallas_call(body, out_shape=jax.ShapeDtypeStruct((64, 128, 128), F32),...  134 us
    pallas_call x1, Pallas kernels, copied(): pl.pallas_call(copy_body, in_specs=[hbm], out_specs=hbm, out_shape=jax.Sh...  3.58 us

profile of v5, /device:TPU:1, one launch (start us, length us, event | category | flops | bytes accessed | tf_op | source)
XLA Modules:
  0.0 139.0 jit_solution(14999123971627627889)
XLA Ops:
  0.0 1.3 select_reduce_fusion
  1.3 134.1 %shard_map.82.src = f32[64,128,128]{2,1,0:T(8,128)} custom-call(f32[8,128,128]{2,1,0:T(8,128)} %bitcast.7, f32[32,8,2,64,128]{4,3,2,1,0:T(8,128)} %bitcast.6, s32[32]{0:T(128)} %bitcast.9, s32[32]{0:T(128)} %local.1, s32[32]{0:T(128)} %aux.1, s32[8,1,128]{2,1,0:T(1,128)} %bitcast.8, s32[32]{0:T(128)} %get-tuple-element.6.first_pair, ...), custom_call_target="tpu_custom_call" | custom-call | flops 20000000000 | bytes 22000000 | tf_op jit(solution)/shard_map/pallas_call | solution.py:481
  135.4 3.6 %shard_map.83 = f32[64,128,128]{2,1,0:T(8,128)} custom-call(f32[64,128,128]{2,1,0:T(8,128)} %shard_map.82.src), custom_call_target="tpu_custom_call" | custom-call | tf_op jit(solution)/shard_map/pallas_call | solution.py:513
